TPU v7x, 32 devices: a whole 2x2x4 slice. The times are simulated.
32 devices in a mesh: section: 2 (over core), seq: 8 (over z, x), mp: 2 (over y).
Axes of the slice: x: 2, y: 2, z: 4, core: 2. Of those that a mesh axis runs over, the one named last changes fastest.
Arguments:
- patches: bfloat16 [4096, 1280], P(('section', 'seq')), may hold values from -6 to 6
- inner_weight: bfloat16 [3, 1280, 1280], P(None, None, 'mp'), may hold values from -0.15625 to 0.15625
- norm_gain: float32 [1280], replicated, may hold values from 0.5 to 12
- outer_weight: bfloat16 [1280, 1280], P('mp'), may hold values from -0.15625 to 0.15625
- merge_gain: float32 [1280], replicated, may hold values from 0.5 to 1.5
- windows: int32 [16, 256], P(('section', 'seq')), may hold values from 0 to 7, never falling along the last dimension, each value on 1 to 64 neighbouring positions
- owners: int32 [1024, 1], P(('section', 'seq')), may hold values from 0 to 15; in each aligned block of 64 rows (0 to 63, 64 to 127, ...) at most 16 rows name the same one
- context_query: bfloat16 [1024, 8192], P('seq', ('section', 'mp')), may hold values from -150 to 150
- context_key: bfloat16 [1024, 1024], P('seq', ('section', 'mp')), may hold values from -6 to 6
- context_value: bfloat16 [1024, 1024], P('seq', ('section', 'mp')), may hold values from -6 to 6
- documents: int32 [1024], replicated, may hold values from 0 to 7, never falling along the last dimension, each value on 1 to 768 neighbouring positions
Outputs:
- delivered: bfloat16 [4096, 5120], P(('section', 'seq'), 'mp')
- attended: bfloat16 [1024, 8192], P('seq', ('section', 'mp'))
Inputs may be any that keep to these rules, and one draw needn't show every extreme that they name: Along each row the window numbers never fall, and each of the 8 windows holds 1 to 64 patches. `owners`: among the 64 tokens of one device (aligned blocks of rows) no owner is named more than 16 times; some owner is named exactly 16 times in some blocks. Document numbers never fall; each of the 8 documents holds 1 to 768 positions, one exactly 768.
All inputs are finite; a program needn't handle non-finite values.
Results may differ from a plain program's by a relative error of at most 0.012.
The roundings to bfloat16 on the way count: a program that leaves them out, or rounds other values in their place, can miss the bound.
Values may be sent and summed in bfloat16 or wider, within the bound.
A program may use at most 128 MiB of HBM per device.

v0:
```python
import math

import jax
import jax.numpy as jnp
from jax import lax
from jax.sharding import PartitionSpec as P

VD = 1280
VH = 16
QH = 64
KVH = 8
HD = 128


EPSILON = 1e-06


def rms_scale(values, gain):
    return values * lax.rsqrt(jnp.mean(values * values, axis=-1, keepdims=True) + EPSILON) * gain


def vision_part(patches, inner_weight, norm_gain, outer_weight, merge_gain, windows):
    patch_rows, feature_width = patches.shape
    head_dim = VD // VH
    local_heads = inner_weight.shape[2] // head_dim
    source = patches.astype(jnp.float32)
    normed = rms_scale(source, norm_gain).astype(jnp.bfloat16)
    query_heads = (
        jnp.dot(normed, inner_weight[0], preferred_element_type=jnp.float32)
        .astype(jnp.bfloat16)
        .reshape(patch_rows, local_heads, head_dim)
    )
    key_heads = (
        jnp.dot(normed, inner_weight[1], preferred_element_type=jnp.float32)
        .astype(jnp.bfloat16)
        .reshape(patch_rows, local_heads, head_dim)
    )
    value_heads = (
        jnp.dot(normed, inner_weight[2], preferred_element_type=jnp.float32)
        .astype(jnp.bfloat16)
        .reshape(patch_rows, local_heads, head_dim)
    )
    scores = jnp.einsum(
        "qhd,khd->hqk", query_heads, key_heads, preferred_element_type=jnp.float32
    ) / math.sqrt(head_dim)
    window_row = windows[0]
    allowed = window_row[:, None] == window_row[None, :]
    scores = jnp.where(allowed[None], scores, -jnp.inf)
    row_peak = jnp.max(scores, axis=-1, keepdims=True)
    weights = jnp.exp(scores - row_peak)
    denominator = jnp.sum(weights, axis=-1)
    context = jnp.einsum(
        "hqk,khd->qhd",
        weights.astype(jnp.bfloat16),
        value_heads,
        preferred_element_type=jnp.float32,
    )
    context = (
        (context / jnp.transpose(denominator)[:, :, None])
        .astype(jnp.bfloat16)
        .reshape(patch_rows, local_heads * head_dim)
    )
    partial_value = jnp.dot(context, outer_weight, preferred_element_type=jnp.float32)
    tokens = patch_rows // 4
    half_count = 4 // lax.axis_size("mp")
    first_patch = lax.axis_index("mp") * half_count
    summed = lax.psum_scatter(
        partial_value.reshape(tokens, 4, feature_width).astype(jnp.bfloat16),
        "mp",
        scatter_dimension=1,
        tiled=True,
    ).astype(jnp.float32)
    residual = (
        lax.dynamic_slice_in_dim(
            source.reshape(tokens, 4, feature_width), first_patch, half_count, 1
        )
        + summed
    )
    merged = rms_scale(residual, merge_gain).astype(jnp.bfloat16)
    return merged.reshape(tokens, half_count * feature_width)


def deliver_tokens(merged, owners):
    tokens = merged.shape[0]
    owner_count = lax.axis_size(("section", "seq"))
    capacity = max(2, 4 * tokens // owner_count)
    target = owners[:, 0]
    order = jnp.arange(tokens, dtype=jnp.int32)
    earlier = (target[:, None] == target[None, :]) & (order[None, :] < order[:, None])
    slot_rank = jnp.sum(earlier, axis=1)
    slot_index = target * capacity + slot_rank
    outgoing = (
        jnp.zeros((owner_count * capacity, merged.shape[1]), jnp.bfloat16)
        .at[slot_index]
        .set(merged)
    )
    arrived = lax.all_to_all(
        outgoing.reshape(owner_count, capacity, merged.shape[1]),
        ("section", "seq"),
        split_axis=0,
        concat_axis=0,
        tiled=True,
    )
    return arrived.reshape(owner_count * capacity, merged.shape[1])


def context_part(context_query, context_key, context_value, documents):
    query_rows = context_query.shape[0]
    kv_heads = context_key.shape[1] // HD
    groups = QH // KVH
    score_scale = 1.0 / math.sqrt(HD)
    query_heads = (
        context_query.reshape(query_rows, kv_heads, groups, HD)
        .transpose(1, 0, 2, 3)
        .reshape(kv_heads, query_rows * groups, HD)
    )
    first_position = lax.axis_index("seq") * query_rows
    query_positions = first_position + jnp.arange(query_rows, dtype=jnp.int32)
    query_docs = lax.dynamic_slice_in_dim(documents, first_position, query_rows, 0)
    row_positions = jnp.repeat(query_positions, groups)
    row_docs = jnp.repeat(query_docs, groups)

    def attend_block(running, key_block, value_block, key_positions, key_docs):
        row_peak, denominator, numerator = running
        scores = (
            jnp.einsum("hrd,khd->hrk", query_heads, key_block, preferred_element_type=jnp.float32)
            * score_scale
        )
        allowed = (key_positions[None, :] <= row_positions[:, None]) & (
            key_docs[None, :] == row_docs[:, None]
        )
        scores = jnp.where(allowed[None], scores, -1e30)
        new_peak = jnp.maximum(row_peak, jnp.max(scores, axis=-1))
        weights = jnp.where(allowed[None], jnp.exp(scores - new_peak[..., None]), 0.0)
        factor = jnp.exp(row_peak - new_peak)
        denominator = denominator * factor + jnp.sum(weights, axis=-1)
        numerator = numerator * factor[..., None] + jnp.einsum(
            "hrk,khd->hrd",
            weights.astype(jnp.bfloat16),
            value_block,
            preferred_element_type=jnp.float32,
        )
        return (new_peak, denominator, numerator)

    start_state = (
        jnp.full((kv_heads, query_rows * groups), -1e30, jnp.float32),
        jnp.zeros((kv_heads, query_rows * groups), jnp.float32),
        jnp.zeros((kv_heads, query_rows * groups, HD), jnp.float32),
    )
    key_local = context_key.reshape(query_rows, kv_heads, HD)
    value_local = context_value.reshape(query_rows, kv_heads, HD)
    key_piece = lax.all_gather(key_local, "seq", axis=0, tiled=True)
    value_piece = lax.all_gather(value_local, "seq", axis=0, tiled=True)
    piece_rows = key_piece.shape[0]
    block_size = math.gcd(piece_rows, 512)
    block_count = piece_rows // block_size
    key_blocks = key_piece.reshape(block_count, block_size, kv_heads, HD)
    value_blocks = value_piece.reshape(block_count, block_size, kv_heads, HD)

    def one_step(carry_state, inputs):
        block_index, key_block, value_block = inputs
        block_start = block_index * block_size
        key_positions = block_start + jnp.arange(block_size, dtype=jnp.int32)
        key_docs = lax.dynamic_slice_in_dim(documents, block_start, block_size, 0)
        return (attend_block(carry_state, key_block, value_block, key_positions, key_docs), None)

    row_peak, denominator, numerator = lax.scan(
        one_step, start_state, (jnp.arange(block_count, dtype=jnp.int32), key_blocks, value_blocks)
    )[0]
    output = (numerator / denominator[..., None]).astype(jnp.bfloat16)
    return (
        output.reshape(kv_heads, query_rows, groups, HD)
        .transpose(1, 0, 2, 3)
        .reshape(query_rows, kv_heads * groups * HD)
    )


def per_device(
    patches,
    inner_weight,
    norm_gain,
    outer_weight,
    merge_gain,
    windows,
    owners,
    context_query,
    context_key,
    context_value,
    documents,
):
    merged = vision_part(patches, inner_weight, norm_gain, outer_weight, merge_gain, windows)
    delivered = deliver_tokens(merged, owners)
    attended = context_part(context_query, context_key, context_value, documents)
    return (delivered, attended)


def solution(mesh):
    in_specs = (
        P(("section", "seq"), None),
        P(None, None, "mp"),
        P(),
        P("mp", None),
        P(),
        P(("section", "seq"), None),
        P(("section", "seq"), None),
        P("seq", ("section", "mp")),
        P("seq", ("section", "mp")),
        P("seq", ("section", "mp")),
        P(),
    )
    out_specs = (P(("section", "seq"), "mp"), P("seq", ("section", "mp")))
    return jax.shard_map(
        per_device, mesh=mesh, in_specs=in_specs, out_specs=out_specs, check_vma=False
    )
```

profile of v0, /device:TPU:0, one launch (start us, length us, event | category | flops | bytes accessed | tf_op | source)
XLA Modules:
  0.0 137.3 jit_solution(3837127901943933100)
XLA Ops:
  7.2 1.4 %multiply_reduce_fusion = f32[256]{0:T(256)S(1)} fusion(bf16[256,1280]{1,0:T(8,128)(2,1)} %param.13), kind=kLoop, calls=%fused_computation.46 | loop fusion | flops 982784 | bytes 656384 | tf_op jit(solution)/shard_map/reduce_sum | solution.py:19
  8.7 2.4 %fusion.43 = bf16[256,640]{1,0:T(8,128)(2,1)S(1)} fusion(bf16[3,1280,640]{2,1,0:T(8,128)(2,1)} %param.14, f32[1280]{0:T(1024)} %param.15, f32[256]{0:T(256)S(1)} %add_rsqrt_fusion.1, bf16[256,1280]{1,0:T(8,128)(2,1)} %param.13), kind=kOutput, calls=%fused_computation.51 | convolution fusion | flops 420904960 | bytes 2630656 | tf_op jit(solution)/shard_map/dot_general | solution.py:29
  11.1 2.2 %fusion.46 = bf16[256,640]{1,0:T(8,128)(2,1)S(1)} fusion(bf16[3,1280,640]{2,1,0:T(8,128)(2,1)} %param.14, f32[1280]{0:T(1024)S(1)} %copy-done.11, f32[256]{0:T(256)S(1)} %add_rsqrt_fusion.1, bf16[256,1280]{1,0:T(8,128)(2,1)S(1)} %copy-done.1), kind=kOutput, calls=%fused_computation.52 | convolution fusion | flops 420904960 | bytes 2627584 | tf_op jit(solution)/shard_map/dot_general | solution.py:34
  13.3 2.9 %fusion.40 = bf16[256,640]{1,0:T(8,128)(2,1)} fusion(bf16[3,1280,640]{2,1,0:T(8,128)(2,1)} %param.14, f32[1280]{0:T(1024)S(1)} %copy-done.11, f32[256]{0:T(256)S(1)} %add_rsqrt_fusion.1, bf16[256,1280]{1,0:T(8,128)(2,1)S(1)} %copy-done.1), kind=kOutput, calls=%fused_computation.50 | convolution fusion | flops 420904960 | bytes 2627584 | tf_op jit(solution)/shard_map/dot_general | solution.py:39
  16.7 1.1 copy.53
  18.8 1.3 fusion.39
  20.1 1.3 copy.57
  22.0 1.5 %convolution_convert_fusion = bf16[64,4,1280]{2,0,1:T(8,128)(2,1)} fusion(bf16[640,1280]{1,0:T(8,128)(2,1)S(1)} %copy-done, bf16[64,4,640]{2,1,0:T(4,128)(2,1)S(1)} %dot_general.31), kind=kOutput, calls=%fused_computation.29 | convolution fusion | flops 419758080 | bytes 2621440 | tf_op jit(solution)/shard_map/dot_general | solution.py:63
  23.6 1.4 reshape.174
  25.2 29.6 %all_gather.7 = bf16[1024,2,128]{0,2,1:T(8,128)(2,1)S(1)} all-gather(bf16[128,2,128]{0,2,1:T(8,128)(2,1)S(1)} %bitcast.119), channel_id=1, replica_groups=mesh['section'=2,'seq'=8,'mp'=2] {'seq'}, dimensions={0}, use_global_device_ids=true | all-gather | bytes 589824 | tf_op jit(solution)/shard_map/all_gather | solution.py:153
  54.8 1.0 copy.64
  55.8 27.9 %all_gather.6 = bf16[1024,2,128]{0,2,1:T(8,128)(2,1)S(1)} all-gather(bf16[128,2,128]{0,2,1:T(8,128)(2,1)S(1)} %bitcast.118), channel_id=1, replica_groups=mesh['section'=2,'seq'=8,'mp'=2] {'seq'}, dimensions={0}, use_global_device_ids=true | all-gather | bytes 589824 | tf_op jit(solution)/shard_map/all_gather | solution.py:152
  84.4 1.6 %constant_dynamic-slice_fusion = f32[64,2,1280]{2,1,0:T(2,128)S(1)} fusion(f32[64,4,1280]{2,1,0:T(4,128)} %reshape.174, s32[]{:T(128)S(6)} %select_n.25), kind=kLoop, calls=%fused_computation.78 | loop fusion | bytes 1310724 | tf_op jit(solution)/shard_map/dynamic_slice | solution.py:74
  86.1 1.1 multiply_reduce_fusion.1
  87.2 1.1 fusion.57
  88.3 0.7 copy.73
  89.1 2.8 %scatter_custom_fusion = bf16[256,2560]{1,0:T(8,128)(2,1)} fusion(s32[64]{0:T(128)S(1)} %fusion.60, bf16[64,2560]{1,0:T(8,128)(2,1)} %bitcast.117, bf16[]{:T(256)} %constant.11.clone.1), kind=kCustom, calls=%fused_computation.61 | custom fusion | bytes 1311232 | tf_op jit(solution)/shard_map/scatter | solution.py:95
  91.8 4.6 %all-to-all-start = ((bf16[16,16,2560]{2,1,0:T(8,128)(2,1)}), bf16[16,16,2560]{2,1,0:T(8,128)(2,1)}, u32[]{:S(2)}, u32[]{:S(2)}) async-start(bf16[16,16,2560]{2,1,0:T(8,128)(2,1)} %bitcast.108), calls=%async_computation.1 | async-start | bytes 2621440 | tf_op jit(solution)/shard_map/all_to_all | solution.py:97
  96.4 15.5 %while.15 = (s32[]{:T(128)}, f32[2,1024]{1,0:T(2,128)S(1)}, f32[2,1024]{1,0:T(2,128)S(1)}, f32[2,1024,128]{2,1,0:T(8,128)}, s32[2]{0:T(128)S(1)}, /*index=5*/s32...) while((s32[]{:T(128)}, f32[2,1024]{1,0:T(2,128)S(1)}, ...), condition=%wide.region_10.11_spmd.clone, body=%wide.region_7.10_spmd.clone.sunk | while | flops 552872448 | bytes 26389796 | solution.py:167
  96.4 0.6 dynamic_slice.43
  98.6 1.0 fusion.78
  99.7 1.1 fusion.80
  100.9 2.3 %fusion.82 = f32[2,1024,128]{2,1,0:T(8,128)S(1)} fusion(f32[2,512,1024]{2,1,0:T(8,128)S(1)} %get-tuple-element.237, f32[2,1024]{1,0:T(2,128)S(1)} %fusion.79, pred[1024,512]{0,1:T(8,128)(4,1)S(1)} %compare_and_fusion.2, f32[2,1024,128]{2,1,0:T(8,128)S(1)} %copy-done.2, f32[2,1024]{1,0:T(2,128)S(1)} %get-tuple-element.239, pred[]{:T(512)S(6)} %compare.3, ...), kind=kOutput, calls=%fused_computation.11.clone.1 | convolution fusion | flops 274464768 | bytes 7094277 | tf_op jit(solution)/shard_map/while/body/eval_jaxpr/hrk,khd->hrd/dot_general | solution.py:137
  103.2 1.0 copy-done.3
  106.4 1.0 fusion.78
  107.4 1.1 fusion.80
  108.6 2.3 %fusion.82 = f32[2,1024,128]{2,1,0:T(8,128)S(1)} fusion(f32[2,512,1024]{2,1,0:T(8,128)S(1)} %get-tuple-element.237, f32[2,1024]{1,0:T(2,128)S(1)} %fusion.79, pred[1024,512]{0,1:T(8,128)(4,1)S(1)} %compare_and_fusion.2, f32[2,1024,128]{2,1,0:T(8,128)S(1)} %copy-done.2, f32[2,1024]{1,0:T(2,128)S(1)} %get-tuple-element.239, pred[]{:T(512)S(6)} %compare.3, ...), kind=kOutput, calls=%fused_computation.11.clone.1 | convolution fusion | flops 274464768 | bytes 7094277 | tf_op jit(solution)/shard_map/while/body/eval_jaxpr/hrk,khd->hrd/dot_general | solution.py:137
  111.0 1.0 copy-done.3
  111.9 1.6 %fusion.56 = bf16[2,128,8,128]{3,2,1,0:T(8,128)(2,1)S(1)} fusion(f32[2,1024,128]{2,1,0:T(8,128)} %get-tuple-element.60, f32[2,1024]{1,0:T(2,128)S(1)} %get-tuple-element.61), kind=kLoop, calls=%fused_computation.65 | loop fusion | flops 524288 | bytes 1581056 | tf_op jit(solution)/shard_map/reshape | solution.py:172
  113.6 0.9 copy.87
  114.5 13.4 %all-to-all-done = bf16[16,16,2560]{2,1,0:T(8,128)(2,1)} async-done(((bf16[16,16,2560]{2,1,0:T(8,128)(2,1)}), bf16[16,16,2560]{2,1,0:T(8,128)(2,1)}, u32[]{:S(2)}, u32[]{:S(2)}) %all-to-all-start) | async-done | bytes 1310752 | tf_op jit(solution)/shard_map/all_to_all | solution.py:97
  128.0 2.5 %copy.102 = bf16[256,2560]{1,0:T(8,128)(2,1)} copy(bf16[256,2560]{1,0:T(8,128)(2,1)} %bitcast.14) | data formatting | bytes 2621440
  (74 shorter events, 5.8 us)
Async XLA Ops:
  7.2 14.8 %copy-start = (bf16[640,1280]{1,0:T(8,128)(2,1)S(1)}, bf16[640,1280]{1,0:T(8,128)(2,1)}, u32[]{:S(2)}) copy-start(bf16[640,1280]{1,0:T(8,128)(2,1)} %param.16) | copy-start | bytes 4915204
  7.2 78.9 %reduce-scatter.2.cloned.1.call-start = ((), (), s32[]{:S(2)}) async-start(), calls=%async_computation.2 | async-start | bytes 983040 | tf_op jit(solution)/shard_map/reduce_scatter | solution.py:67
  8.6 2.5 %copy-start.1 = (bf16[256,1280]{1,0:T(8,128)(2,1)S(1)}, bf16[256,1280]{1,0:T(8,128)(2,1)}, u32[]{:S(2)}) copy-start(bf16[256,1280]{1,0:T(8,128)(2,1)} %param.13) | copy-start | bytes 1966084
  8.6 2.5 %copy-start.11 = (f32[1280]{0:T(1024)S(1)}, f32[1280]{0:T(1024)}, u32[]{:S(2)}) copy-start(f32[1280]{0:T(1024)} %param.15) | copy-start | bytes 15364
  13.3 2.9 %copy-start.10 = (s32[1,256]{1,0:T(1,128)S(1)}, s32[1,256]{1,0:T(1,128)}, u32[]{:S(2)}) copy-start(s32[1,256]{1,0:T(1,128)} %param.18) | copy-start | bytes 3076
  22.0 3.0 %copy-start.6 = (bf16[128,256]{1,0:T(8,128)(2,1)S(1)}, bf16[128,256]{1,0:T(8,128)(2,1)}, u32[]{:S(2)}) copy-start(bf16[128,256]{1,0:T(8,128)(2,1)} %param.21) | copy-start | bytes 196612
  22.0 3.1 %copy-start.7 = (bf16[128,256]{1,0:T(8,128)(2,1)S(1)}, bf16[128,256]{1,0:T(8,128)(2,1)}, u32[]{:S(2)}) copy-start(bf16[128,256]{1,0:T(8,128)(2,1)} %param.22) | copy-start | bytes 196612
  25.0 59.0 %copy-start.4 = (bf16[128,2048]{1,0:T(8,128)(2,1)S(1)}, bf16[128,2048]{1,0:T(8,128)(2,1)}, u32[]{:S(2)}) copy-start(bf16[128,2048]{1,0:T(8,128)(2,1)} %param.20) | copy-start | bytes 1572868
  55.8 28.4 %copy-start.8 = (s32[1024]{0:T(1024)S(1)}, s32[1024]{0:T(1024)}, u32[]{:S(2)}) copy-start(s32[1024]{0:T(1024)} %param.23) | copy-start | bytes 12292
  55.8 28.5 %copy-start.12 = (s32[64,1]{0,1:T(1,128)S(1)}, s32[64,1]{0,1:T(1,128)}, u32[]{:S(2)}) copy-start(s32[64,1]{0,1:T(1,128)} %param.19) | copy-start | bytes 772
  84.0 3.3 %copy-start.9 = (f32[1280]{0:T(1024)S(1)}, f32[1280]{0:T(1024)}, u32[]{:S(2)}) copy-start(f32[1280]{0:T(1024)} %param.17) | copy-start | bytes 15364
  89.1 7.3 %copy-start.5 = (bf16[1024,2,128]{2,0,1:T(8,128)(2,1)S(1)}, bf16[1024,2,128]{2,0,1:T(8,128)(2,1)}, u32[]{:S(2)}) copy-start(bf16[1024,2,128]{2,0,1:T(8,128)(2,1)} %copy.64) | copy-start | bytes 1572868
  91.8 36.1 %all-to-all-start = ((bf16[16,16,2560]{2,1,0:T(8,128)(2,1)}), bf16[16,16,2560]{2,1,0:T(8,128)(2,1)}, u32[]{:S(2)}, u32[]{:S(2)}) async-start(bf16[16,16,2560]{2,1,0:T(8,128)(2,1)} %bitcast.108), calls=%async_computation.1 | async-start | bytes 2621440 | tf_op jit(solution)/shard_map/all_to_all | solution.py:97
  99.6 1.2 copy-start.2
  103.2 1.0 copy-start.3
  107.4 1.2 copy-start.2
  110.9 1.0 copy-start.3
Sparse Core Ops, SparseCore 0:
  23.7 18.6 reduce-scatter.1
where the time goes:
time: 138 us; the launch traced here: 137 us
  blocking collectives  57.5 us (42%)
  local copies, waits for them, and re-layouts  19.2 us (14%)
  matrix products  17.5 us (13%)
  between operations  14.3 us (10%)
  waiting for transfers between devices  13.5 us (10%)
  other arithmetic  9.24 us (7%)
  starting transfers between devices  4.6 us (3%)
  loops' own time  1.47 us (1%)
    all_gather x1, blocking collectives, context_part(): value_piece = lax.all_gather(value_local, 'seq', axis=0, tiled=True)  29.6 us
    all_gather x1, blocking collectives, context_part(): key_piece = lax.all_gather(key_local, 'seq', axis=0, tiled=True)  27.9 us
    all_to_all x1, waiting for transfers between devices, deliver_tokens(): lax.all_to_all(outgoing.reshape(owner_count, capacity, merged.shape[1]),...  13.4 us
    dot_general x2, matrix products, attend_block(): jnp.einsum('hrk,khd->hrd', weights.astype(jnp.bfloat16), value_block, pre...  4.63 us
    all_to_all x1, starting transfers between devices, deliver_tokens(): lax.all_to_all(outgoing.reshape(owner_count, capacity, merged.shape[1]),...  4.56 us
    unnamed x27, local copies, waits for them, and re-layouts  3.78 us
    dot_general x1, matrix products, vision_part(): jnp.dot(normed, inner_weight[2], preferred_element_type=jnp.float32)  2.88 us
  transfers between devices with their start and end apart: 2, of which 1 were waited for; matrix products, arithmetic and copies ran while one was open for 14% of the time, Pallas kernels for 0%

commit v1 on v0

v1 whole, which is shorter than its diff:
```python
import functools
import math

import jax
import jax.numpy as jnp
from jax import lax
from jax.experimental import pallas as pl
from jax.experimental.pallas import tpu as pltpu
from jax.sharding import PartitionSpec as P

VD = 1280
VH = 16
QH = 64
KVH = 8
HD = 128
EPSILON = 1e-06
LOG2E = 1.4426950408889634
MESH = pl.DeviceIdType.MESH
F32 = jnp.float32
BF16 = jnp.bfloat16


def rms_scale(values, gain):
    return values * lax.rsqrt(jnp.mean(values * values, axis=-1, keepdims=True) + EPSILON) * gain


def row_to_column(row, size):
    spread = jnp.broadcast_to(row, (size, size))
    eye = lax.broadcasted_iota(jnp.int32, (size, size), 0) == lax.broadcasted_iota(
        jnp.int32, (size, size), 1
    )
    return jnp.sum(jnp.where(eye, spread, 0.0), axis=1, keepdims=True)


def kernel(
    sections,
    seqs,
    capacity,
    patches_ref,
    inner_hbm,
    norm_ref,
    outer_hbm,
    merge_ref,
    window_ref,
    owner_ref,
    query_hbm,
    key_hbm,
    value_hbm,
    doc_ref,
    delivered_hbm,
    attended_ref,
    inner_buf,
    outer_buf,
    query_buf,
    kv,
    normed_buf,
    qkv_buf,
    ctx_buf,
    part_send,
    part_recv,
    outgoing,
    load_sem,
    kv_recv,
    chain_send,
    side_send,
    part_sem,
    out_send,
    out_recv,
):
    section, seq, mp = lax.axis_index("section"), lax.axis_index("seq"), lax.axis_index("mp")
    owner_count = sections * seqs
    me = section * seqs + seq
    rows = patches_ref.shape[0]
    width = patches_ref.shape[1]
    tokens = rows // 4
    head_dim = VD // VH
    local = inner_hbm.shape[2]
    local_heads = local // head_dim
    half = rows // 2

    def at(sec, sq, m):
        return {"section": sec, "seq": sq, "mp": m}

    loads = [
        pltpu.make_async_copy(key_hbm, kv.at[seq, 0], load_sem.at[0]),
        pltpu.make_async_copy(value_hbm, kv.at[seq, 1], load_sem.at[1]),
        pltpu.make_async_copy(inner_hbm.at[0], inner_buf.at[0], load_sem.at[2]),
        pltpu.make_async_copy(inner_hbm.at[1], inner_buf.at[1], load_sem.at[3]),
        pltpu.make_async_copy(inner_hbm.at[2], inner_buf.at[2], load_sem.at[4]),
        pltpu.make_async_copy(outer_hbm, outer_buf, load_sem.at[5]),
        pltpu.make_async_copy(query_hbm, query_buf, load_sem.at[6]),
    ]
    for load in loads:
        load.start()

    barrier = pltpu.get_barrier_semaphore()

    def greet(k, carry):
        other = lax.rem(me + k, owner_count)
        pl.semaphore_signal(
            barrier,
            inc=1,
            device_id=at(other // seqs, lax.rem(other, seqs), mp),
            device_id_type=MESH,
        )
        return carry

    lax.fori_loop(1, owner_count, greet, 0)
    pl.semaphore_signal(
        barrier, inc=1, device_id=at(section, seq, 1 - mp), device_id_type=MESH
    )

    def clear(j, carry):
        kv[j] = jnp.zeros(kv.shape[1:], BF16)
        return carry

    lax.fori_loop(seq + 1, seqs, clear, 0)

    pl.semaphore_wait(barrier, owner_count)

    side = seq + 1 - 2 * lax.rem(seq, 2)

    def chain_copy(j):
        block = seq - 2 * j
        return pltpu.make_async_remote_copy(
            src_ref=kv.at[block],
            dst_ref=kv.at[block],
            send_sem=chain_send.at[j],
            recv_sem=kv_recv.at[block],
            device_id=at(section, seq + 2, mp),
            device_id_type=MESH,
        )

    def side_copy(j):
        block = seq - 2 * j
        return pltpu.make_async_remote_copy(
            src_ref=kv.at[block],
            dst_ref=kv.at[block],
            send_sem=side_send.at[j],
            recv_sem=kv_recv.at[block],
            device_id=at(section, side, mp),
            device_id_type=MESH,
        )

    def arrived(block):
        return pltpu.make_async_copy(kv.at[block], kv.at[block], kv_recv.at[block])

    loads[0].wait()
    loads[1].wait()

    @pl.when(seq + 2 < seqs)
    def _():
        chain_copy(0).start()

    @pl.when(lax.rem(seq, 2) == 0)
    def _():
        side_copy(0).start()

    def relay(j, carry):
        @pl.when(seq - 2 * j >= 0)
        def _():
            arrived(seq - 2 * j).wait()

            @pl.when(seq + 2 < seqs)
            def _():
                chain_copy(j).start()

            side_copy(j).start()

        return carry

    hops = seqs // 2
    first_hops = 1 + (hops - 1) // 3
    second_hops = 1 + 2 * (hops - 1) // 3

    normed_buf[...] = rms_scale(patches_ref[...].astype(F32), norm_ref[...]).astype(BF16)
    for i in range(3):
        loads[2 + i].wait()
        qkv_buf[i] = jnp.dot(
            normed_buf[...], inner_buf[i], preferred_element_type=F32
        ).astype(BF16)

    lax.fori_loop(1, first_hops, relay, 0)

    window_row = window_ref[...].astype(F32)
    allowed = row_to_column(window_row, rows) == window_row
    score_scale = LOG2E / math.sqrt(head_dim)
    ctx = [jnp.zeros((rows, 128), F32) for _ in range(local // 128)]
    for h in range(local_heads):
        low, high = h * head_dim, (h + 1) * head_dim
        first, last = low // 128, -(-high // 128)
        span = pl.ds(first * 128, (last - first) * 128)
        lanes = first * 128 + lax.broadcasted_iota(jnp.int32, (1, (last - first) * 128), 1)
        inside = (lanes >= low) & (lanes < high)
        query = jnp.where(inside, qkv_buf[0, :, span], jnp.zeros((), BF16))
        scores = lax.dot_general(
            query, qkv_buf[1, :, span], (((1,), (1,)), ((), ())), preferred_element_type=F32
        )
        scores = jnp.where(allowed, scores, -jnp.inf)
        peak = jnp.max(scores, axis=-1, keepdims=True)
        weights = jnp.exp2((scores - peak) * score_scale)
        denominator = jnp.sum(weights, axis=-1, keepdims=True)
        part = jnp.dot(weights.astype(BF16), qkv_buf[2, :, span], preferred_element_type=F32)
        part = jnp.where(inside, part / denominator, 0.0)
        for i in range(first, last):
            ctx[i] = ctx[i] + part[:, (i - first) * 128 : (i - first + 1) * 128]
    for i in range(local // 128):
        ctx_buf[:, i * 128 : (i + 1) * 128] = ctx[i].astype(BF16)

    lax.fori_loop(first_hops, second_hops, relay, 0)

    place = lax.broadcasted_iota(jnp.int32, (half, rows), 0)
    source_at = lax.broadcasted_iota(jnp.int32, (half, rows), 1)

    def chosen(m):
        wanted = 4 * lax.rem(place, tokens) + 2 * m + place // tokens
        return jnp.where(source_at == wanted, 1.0, 0.0).astype(BF16)

    loads[5].wait()
    theirs = jnp.dot(chosen(1 - mp), ctx_buf[...], preferred_element_type=F32).astype(BF16)
    part_send[...] = jnp.dot(theirs, outer_buf[...], preferred_element_type=F32).astype(BF16)
    part_copy = pltpu.make_async_remote_copy(
        src_ref=part_send,
        dst_ref=part_recv,
        send_sem=part_sem.at[0],
        recv_sem=part_sem.at[1],
        device_id=at(section, seq, 1 - mp),
        device_id_type=MESH,
    )
    part_copy.start()
    pick = chosen(mp)
    ours = jnp.dot(pick, ctx_buf[...], preferred_element_type=F32).astype(BF16)
    own_part = jnp.dot(ours, outer_buf[...], preferred_element_type=F32)
    own_part = own_part + jnp.dot(pick, patches_ref[...], preferred_element_type=F32)

    owner_spread = jnp.broadcast_to(owner_ref[...].astype(F32), (tokens, tokens))
    earlier_at = lax.broadcasted_iota(jnp.int32, (tokens, tokens), 0)
    later_at = lax.broadcasted_iota(jnp.int32, (tokens, tokens), 1)
    owner_row = jnp.sum(
        jnp.where(earlier_at == later_at, owner_spread, 0.0), axis=0, keepdims=True
    )
    rank_row = jnp.sum(
        jnp.where((owner_spread == owner_row) & (earlier_at < later_at), 1.0, 0.0),
        axis=0,
        keepdims=True,
    )
    slot_row = (owner_row * capacity + rank_row).astype(jnp.int32)
    slot_at = lax.broadcasted_iota(jnp.int32, (capacity, tokens), 0)

    lax.fori_loop(second_hops, hops, relay, 0)

    part_copy.wait_recv()
    residual = own_part + part_recv[...].astype(F32)
    normed_buf[0:half, :] = rms_scale(residual, merge_ref[...]).astype(BF16)

    def out_copy(owner):
        return pltpu.make_async_remote_copy(
            src_ref=outgoing.at[owner],
            dst_ref=delivered_hbm.at[me],
            send_sem=out_send.at[owner],
            recv_sem=out_recv.at[me],
            device_id=at(owner // seqs, lax.rem(owner, seqs), mp),
            device_id_type=MESH,
        )

    def fill(owner):
        spot = jnp.where(slot_at + owner * capacity == slot_row, 1.0, 0.0).astype(BF16)
        for g in range(2):
            outgoing[owner, :, g * width : (g + 1) * width] = jnp.dot(
                spot,
                normed_buf[g * tokens : (g + 1) * tokens, :],
                preferred_element_type=F32,
            ).astype(BF16)

    def send_out(k, carry):
        owner = lax.rem(me + k, owner_count)
        fill(owner)
        out_copy(owner).start()
        return carry

    lax.fori_loop(1, owner_count, send_out, 0)
    fill(me)
    keep = pltpu.make_async_copy(outgoing.at[me], delivered_hbm.at[me], out_send.at[me])
    keep.start()

    def side_arrival(j, carry):
        block = side - 2 * j

        @pl.when((block >= 0) & (block < seq))
        def _():
            arrived(block).wait()

        return carry

    lax.fori_loop(0, hops, side_arrival, 0)
    loads[6].wait()

    query_rows = query_buf.shape[0]
    context = doc_ref.shape[1]
    groups = QH // KVH
    heads = query_buf.shape[1] // HD
    together = max(1, min(4, (512 * 1024) // (query_rows * context)))
    first_position = pl.multiple_of(seq * query_rows, query_rows)
    key_docs = doc_ref[...].astype(F32)
    query_docs = row_to_column(
        doc_ref[:, pl.ds(first_position, query_rows)].astype(F32), query_rows
    )
    key_at = lax.broadcasted_iota(jnp.int32, (query_rows, context), 1)
    query_at = first_position + lax.broadcasted_iota(jnp.int32, (query_rows, context), 0)
    open_pairs = jnp.where((key_at <= query_at) & (query_docs == key_docs), 0.0, -jnp.inf)
    context_scale = LOG2E / math.sqrt(HD)

    def attend(i, carry):
        kv_lanes = pl.ds(pl.multiple_of(i * together // groups * HD, HD), HD)
        keys = kv[:, 0, :, kv_lanes].reshape(context, HD)
        values = kv[:, 1, :, kv_lanes].reshape(context, HD)
        lanes = [
            pl.ds(pl.multiple_of((i * together + u) * HD, HD), HD) for u in range(together)
        ]
        queries = jnp.concatenate([query_buf[:, lane] for lane in lanes], axis=0)
        scores = lax.dot_general(
            queries, keys, (((1,), (1,)), ((), ())), preferred_element_type=F32
        )
        scores = scores.reshape(together, query_rows, context) + open_pairs[None]
        peak = jnp.max(scores, axis=-1, keepdims=True)
        weights = jnp.exp2((scores - peak) * context_scale)
        denominator = jnp.sum(weights, axis=-1, keepdims=True)
        output = jnp.dot(
            weights.astype(BF16).reshape(together * query_rows, context),
            values,
            preferred_element_type=F32,
        ).reshape(together, query_rows, HD)
        output = (output / denominator).astype(BF16)
        for u in range(together):
            attended_ref[:, lanes[u]] = output[u]
        return carry

    lax.fori_loop(0, heads // together, attend, 0)

    part_copy.wait_send()

    def finish_kv(j, carry):
        @pl.when((seq - 2 * j >= 0) & (seq + 2 < seqs))
        def _():
            chain_copy(j).wait_send()

        @pl.when((seq - 2 * j >= 0) & (seq - 2 * j < side))
        def _():
            side_copy(j).wait_send()

        return carry

    lax.fori_loop(0, hops, finish_kv, 0)
    keep.wait()

    def finish_out(k, carry):
        owner = lax.rem(me + k, owner_count)
        out_copy(owner).wait_send()
        pltpu.make_async_copy(
            outgoing.at[owner], delivered_hbm.at[owner], out_recv.at[owner]
        ).wait()
        return carry

    lax.fori_loop(1, owner_count, finish_out, 0)


def per_device(
    patches,
    inner_weight,
    norm_gain,
    outer_weight,
    merge_gain,
    windows,
    owners,
    context_query,
    context_key,
    context_value,
    documents,
):
    sections, seqs = lax.axis_size("section"), lax.axis_size("seq")
    owner_count = sections * seqs
    rows, width = patches.shape
    tokens = rows // 4
    capacity = max(2, 4 * tokens // owner_count)
    local = inner_weight.shape[2]
    query_rows, query_width = context_query.shape
    kv_width = context_key.shape[1]
    vmem = pl.BlockSpec(memory_space=pltpu.VMEM)
    anywhere = pl.BlockSpec(memory_space=pl.ANY)
    hops = seqs // 2
    delivered, attended = pl.pallas_call(
        functools.partial(kernel, sections, seqs, capacity),
        out_shape=(
            jax.ShapeDtypeStruct((owner_count, capacity, 2 * width), BF16),
            jax.ShapeDtypeStruct((query_rows, query_width), BF16),
        ),
        in_specs=[
            vmem,
            anywhere,
            vmem,
            anywhere,
            vmem,
            vmem,
            vmem,
            anywhere,
            anywhere,
            anywhere,
            vmem,
        ],
        out_specs=(anywhere, vmem),
        scratch_shapes=[
            pltpu.VMEM((3, width, local), BF16),
            pltpu.VMEM((local, width), BF16),
            pltpu.VMEM((query_rows, query_width), BF16),
            pltpu.VMEM((seqs, 2, query_rows, kv_width), BF16),
            pltpu.VMEM((rows, width), BF16),
            pltpu.VMEM((3, rows, local), BF16),
            pltpu.VMEM((rows, local), BF16),
            pltpu.VMEM((rows // 2, width), BF16),
            pltpu.VMEM((rows // 2, width), BF16),
            pltpu.VMEM((owner_count, capacity, 2 * width), BF16),
            pltpu.SemaphoreType.DMA((7,)),
            pltpu.SemaphoreType.DMA((seqs,)),
            pltpu.SemaphoreType.DMA((hops,)),
            pltpu.SemaphoreType.DMA((hops,)),
            pltpu.SemaphoreType.DMA((2,)),
            pltpu.SemaphoreType.DMA((owner_count,)),
            pltpu.SemaphoreType.DMA((owner_count,)),
        ],
        compiler_params=pltpu.CompilerParams(
            collective_id=0, has_side_effects=True, vmem_limit_bytes=56 * 1024 * 1024
        ),
    )(
        patches,
        inner_weight,
        norm_gain.reshape(1, width),
        outer_weight,
        merge_gain.reshape(1, width),
        windows,
        owners,
        context_query,
        context_key,
        context_value,
        documents.reshape(1, -1),
    )
    return delivered.reshape(owner_count * capacity, 2 * width), attended


def solution(mesh):
    in_specs = (
        P(("section", "seq"), None),
        P(None, None, "mp"),
        P(),
        P("mp", None),
        P(),
        P(("section", "seq"), None),
        P(("section", "seq"), None),
        P("seq", ("section", "mp")),
        P("seq", ("section", "mp")),
        P("seq", ("section", "mp")),
        P(),
    )
    out_specs = (P(("section", "seq"), "mp"), P("seq", ("section", "mp")))
    return jax.shard_map(
        per_device, mesh=mesh, in_specs=in_specs, out_specs=out_specs, check_vma=False
    )
```

time: 138 us -> 61.5 us (0.45)
  the two profiles are of different devices: /device:TPU:0 before, /device:TPU:11 now
where the time goes in v1:
time: 61.5 us; the launch traced here: 61.2 us
  Pallas kernels  53.3 us (87%)
  local copies, waits for them, and re-layouts  7.25 us (12%)
  between operations  0.65 us (1%)
    pallas_call x1, Pallas kernels, per_device(): pl.pallas_call(functools.partial(kernel, sections, seqs, capacity), out_s...  53.3 us
    unnamed x5, local copies, waits for them, and re-layouts  4.67 us
    reshape x1, local copies, waits for them, and re-layouts, per_device(): norm_gain.reshape(1, width)  1.29 us
    reshape x1, local copies, waits for them, and re-layouts, per_device(): merge_gain.reshape(1, width)  1.29 us

profile of v1, /device:TPU:11, one launch (start us, length us, event | category | flops | bytes accessed | tf_op | source)
XLA Modules:
  0.0 61.2 jit_solution(3526149396992404773)
XLA Ops:
  0.6 1.3 %reshape.16.norm_ref = f32[1,1280]{1,0:T(1,128)} reshape(f32[1280]{0:T(1024)} %param.13) | data formatting | bytes 10240 | tf_op jit(solution)/shard_map/reshape | solution.py:436
  1.9 1.3 %reshape.17.merge_ref = f32[1,1280]{1,0:T(1,128)} reshape(f32[1280]{0:T(1024)} %param.15) | data formatting | bytes 10240 | tf_op jit(solution)/shard_map/reshape | solution.py:438
  3.2 1.4 %copy.13.owner_ref = s32[64,1]{1,0:T(8,128)} copy(s32[64,1]{0,1:T(1,128)} %param.17) | data formatting | bytes 512 | tf_op args[6]
  4.6 53.3 %shard_map.122 = (bf16[16,16,2560]{2,1,0:T(8,128)(2,1)}, bf16[128,2048]{1,0:T(8,128)(2,1)}) custom-call(bf16[256,1280]{1,0:T(8,128)(2,1)} %patches_ref.1, bf16[3,1280,640]{2,1,0:T(8,128)(2,1)} %inner_hbm.1, f32[1,1280]{1,0:T(1,128)} %reshape.16.norm_ref, bf16[640,1280]{1,0:T(8,128)(2,1)} %outer_hbm.1, f32[1,1280]{1,0:T(1,128)} %reshape.17.merge_ref, ...), custom_call_target="tpu_custom_call" | custom-call | tf_op jit(solution)/shard_map/pallas_call | solution.py:391
  57.9 0.0 copy-start
  57.9 2.5 %copy.16 = bf16[256,2560]{1,0:T(8,128)(2,1)} copy(bf16[256,2560]{1,0:T(8,128)(2,1)} %bitcast.2) | data formatting | bytes 2621440
  60.4 0.0 copy-done
  60.4 0.8 %copy.17 = bf16[128,2048]{1,0:T(8,128)(2,1)} copy(bf16[128,2048]{1,0:T(8,128)(2,1)S(1)} %copy-done) | data formatting | bytes 1048576
Async XLA Ops:
  57.9 2.5 %copy-start = (bf16[128,2048]{1,0:T(8,128)(2,1)S(1)}, bf16[128,2048]{1,0:T(8,128)(2,1)}, u32[]{:S(2)}) copy-start(bf16[128,2048]{1,0:T(8,128)(2,1)} %get-tuple-element.9) | copy-start | bytes 1572868

commit v2 on v1

--- a/solution.py
+++ b/solution.py
@@ -173,7 +173,7 @@
     first_hops = 1 + (hops - 1) // 3
     second_hops = 1 + 2 * (hops - 1) // 3
 
-    normed_buf[...] = rms_scale(patches_ref[...].astype(F32), norm_ref[...]).astype(BF16)
+    normed_buf[...] = rms_scale(patches_ref[...].astype(F32), norm_ref[...].reshape(1, width)).astype(BF16)
     for i in range(3):
         loads[2 + i].wait()
         qkv_buf[i] = jnp.dot(
@@ -217,28 +217,32 @@
         return jnp.where(source_at == wanted, 1.0, 0.0).astype(BF16)
 
     loads[5].wait()
-    theirs = jnp.dot(chosen(1 - mp), ctx_buf[...], preferred_element_type=F32).astype(BF16)
-    part_send[...] = jnp.dot(theirs, outer_buf[...], preferred_element_type=F32).astype(BF16)
-    part_copy = pltpu.make_async_remote_copy(
-        src_ref=part_send,
-        dst_ref=part_recv,
-        send_sem=part_sem.at[0],
-        recv_sem=part_sem.at[1],
-        device_id=at(section, seq, 1 - mp),
-        device_id_type=MESH,
-    )
-    part_copy.start()
+    their_pick = chosen(1 - mp)
+    theirs = jnp.dot(their_pick, ctx_buf[...], preferred_element_type=F32).astype(BF16)
+    part_copies = []
+    for g in range(2):
+        part_send[g] = jnp.dot(
+            theirs[g * tokens : (g + 1) * tokens], outer_buf[...], preferred_element_type=F32
+        ).astype(BF16)
+        part_copy = pltpu.make_async_remote_copy(
+            src_ref=part_send.at[g],
+            dst_ref=part_recv.at[g],
+            send_sem=part_sem.at[0, g],
+            recv_sem=part_sem.at[1, g],
+            device_id=at(section, seq, 1 - mp),
+            device_id_type=MESH,
+        )
+        part_copy.start()
+        part_copies.append(part_copy)
     pick = chosen(mp)
     ours = jnp.dot(pick, ctx_buf[...], preferred_element_type=F32).astype(BF16)
     own_part = jnp.dot(ours, outer_buf[...], preferred_element_type=F32)
     own_part = own_part + jnp.dot(pick, patches_ref[...], preferred_element_type=F32)
 
-    owner_spread = jnp.broadcast_to(owner_ref[...].astype(F32), (tokens, tokens))
+    owner_row = owner_ref[...].astype(F32)
+    owner_spread = row_to_column(owner_row, tokens)
     earlier_at = lax.broadcasted_iota(jnp.int32, (tokens, tokens), 0)
     later_at = lax.broadcasted_iota(jnp.int32, (tokens, tokens), 1)
-    owner_row = jnp.sum(
-        jnp.where(earlier_at == later_at, owner_spread, 0.0), axis=0, keepdims=True
-    )
     rank_row = jnp.sum(
         jnp.where((owner_spread == owner_row) & (earlier_at < later_at), 1.0, 0.0),
         axis=0,
@@ -249,39 +253,47 @@
 
     lax.fori_loop(second_hops, hops, relay, 0)
 
-    part_copy.wait_recv()
-    residual = own_part + part_recv[...].astype(F32)
-    normed_buf[0:half, :] = rms_scale(residual, merge_ref[...]).astype(BF16)
-
-    def out_copy(owner):
+    def out_copy(owner, g):
         return pltpu.make_async_remote_copy(
-            src_ref=outgoing.at[owner],
-            dst_ref=delivered_hbm.at[me],
-            send_sem=out_send.at[owner],
-            recv_sem=out_recv.at[me],
+            src_ref=outgoing.at[g, owner],
+            dst_ref=delivered_hbm.at[me, :, pl.ds(g * width, width)],
+            send_sem=out_send.at[g, owner],
+            recv_sem=out_recv.at[g, me],
             device_id=at(owner // seqs, lax.rem(owner, seqs), mp),
             device_id_type=MESH,
         )
 
-    def fill(owner):
+    def fill(owner, g):
         spot = jnp.where(slot_at + owner * capacity == slot_row, 1.0, 0.0).astype(BF16)
-        for g in range(2):
-            outgoing[owner, :, g * width : (g + 1) * width] = jnp.dot(
-                spot,
-                normed_buf[g * tokens : (g + 1) * tokens, :],
-                preferred_element_type=F32,
-            ).astype(BF16)
-
-    def send_out(k, carry):
-        owner = lax.rem(me + k, owner_count)
-        fill(owner)
-        out_copy(owner).start()
-        return carry
-
-    lax.fori_loop(1, owner_count, send_out, 0)
-    fill(me)
-    keep = pltpu.make_async_copy(outgoing.at[me], delivered_hbm.at[me], out_send.at[me])
-    keep.start()
+        outgoing[g, owner] = jnp.dot(
+            spot,
+            normed_buf[g * tokens : (g + 1) * tokens, :],
+            preferred_element_type=F32,
+        ).astype(BF16)
+
+    keeps = []
+    for g in range(2):
+        part_copies[g].wait_recv()
+        residual = own_part[g * tokens : (g + 1) * tokens] + part_recv[g].astype(F32)
+        normed_buf[g * tokens : (g + 1) * tokens, :] = rms_scale(
+            residual, merge_ref[...].reshape(1, width)
+        ).astype(BF16)
+
+        def send_out(k, carry):
+            owner = lax.rem(me + k, owner_count)
+            fill(owner, g)
+            out_copy(owner, g).start()
+            return carry
+
+        lax.fori_loop(1, owner_count, send_out, 0)
+        fill(me, g)
+        keep = pltpu.make_async_copy(
+            outgoing.at[g, me],
+            delivered_hbm.at[me, :, pl.ds(g * width, width)],
+            out_send.at[g, me],
+        )
+        keep.start()
+        keeps.append(keep)
 
     def side_arrival(j, carry):
         block = side - 2 * j
@@ -337,7 +349,8 @@
 
     lax.fori_loop(0, heads // together, attend, 0)
 
-    part_copy.wait_send()
+    for part_copy in part_copies:
+        part_copy.wait_send()
 
     def finish_kv(j, carry):
         @pl.when((seq - 2 * j >= 0) & (seq + 2 < seqs))
@@ -351,14 +364,18 @@
         return carry
 
     lax.fori_loop(0, hops, finish_kv, 0)
-    keep.wait()
+    for keep in keeps:
+        keep.wait()
 
     def finish_out(k, carry):
         owner = lax.rem(me + k, owner_count)
-        out_copy(owner).wait_send()
-        pltpu.make_async_copy(
-            outgoing.at[owner], delivered_hbm.at[owner], out_recv.at[owner]
-        ).wait()
+        for g in range(2):
+            out_copy(owner, g).wait_send()
+            pltpu.make_async_copy(
+                outgoing.at[g, owner],
+                delivered_hbm.at[owner, :, pl.ds(g * width, width)],
+                out_recv.at[g, owner],
+            ).wait()
         return carry
 
     lax.fori_loop(1, owner_count, finish_out, 0)
@@ -416,16 +433,16 @@
             pltpu.VMEM((rows, width), BF16),
             pltpu.VMEM((3, rows, local), BF16),
             pltpu.VMEM((rows, local), BF16),
-            pltpu.VMEM((rows // 2, width), BF16),
-            pltpu.VMEM((rows // 2, width), BF16),
-            pltpu.VMEM((owner_count, capacity, 2 * width), BF16),
+            pltpu.VMEM((2, tokens, width), BF16),
+            pltpu.VMEM((2, tokens, width), BF16),
+            pltpu.VMEM((2, owner_count, capacity, width), BF16),
             pltpu.SemaphoreType.DMA((7,)),
             pltpu.SemaphoreType.DMA((seqs,)),
             pltpu.SemaphoreType.DMA((hops,)),
             pltpu.SemaphoreType.DMA((hops,)),
-            pltpu.SemaphoreType.DMA((2,)),
-            pltpu.SemaphoreType.DMA((owner_count,)),
-            pltpu.SemaphoreType.DMA((owner_count,)),
+            pltpu.SemaphoreType.DMA((2, 2)),
+            pltpu.SemaphoreType.DMA((2, owner_count)),
+            pltpu.SemaphoreType.DMA((2, owner_count)),
         ],
         compiler_params=pltpu.CompilerParams(
             collective_id=0, has_side_effects=True, vmem_limit_bytes=56 * 1024 * 1024
@@ -433,11 +450,11 @@
     )(
         patches,
         inner_weight,
-        norm_gain.reshape(1, width),
+        norm_gain,
         outer_weight,
-        merge_gain.reshape(1, width),
+        merge_gain,
         windows,
-        owners,
+        owners.reshape(1, tokens),
         context_query,
         context_key,
         context_value,

time: 61.5 us -> 54.9 us (0.89)
  the two profiles are of different devices: /device:TPU:11 before, /device:TPU:0 now
where the time goes in v2:
time: 54.9 us; the launch traced here: 54.7 us
  Pallas kernels  50.8 us (93%)
  local copies, waits for them, and re-layouts  3.31 us (6%)
  between operations  0.65 us (1%)
    pallas_call x1, Pallas kernels, per_device(): pl.pallas_call(functools.partial(kernel, sections, seqs, capacity), out_s...  50.8 us
    unnamed x4, local copies, waits for them, and re-layouts  3.31 us

profile of v2, /device:TPU:0, one launch (start us, length us, event | category | flops | bytes accessed | tf_op | source)
XLA Modules:
  0.0 54.7 jit_solution(11373563331907016224)
XLA Ops:
  0.6 50.8 %shard_map.122 = (bf16[16,16,2560]{2,1,0:T(8,128)(2,1)}, bf16[128,2048]{1,0:T(8,128)(2,1)}) custom-call(bf16[256,1280]{1,0:T(8,128)(2,1)} %patches_ref.1, bf16[3,1280,640]{2,1,0:T(8,128)(2,1)} %inner_hbm.1, f32[1280]{0:T(1024)} %norm_ref.1, bf16[640,1280]{1,0:T(8,128)(2,1)} %outer_hbm.1, f32[1280]{0:T(1024)} %merge_ref.1, s32[1,256]{1,0:T(1,128)} %window_ref.1, ...), custom_call_target="tpu_custom_call" | custom-call | tf_op jit(solution)/shard_map/pallas_call | solution.py:408
  51.4 0.0 copy-start
  51.4 2.5 %copy.15 = bf16[256,2560]{1,0:T(8,128)(2,1)} copy(bf16[256,2560]{1,0:T(8,128)(2,1)} %bitcast.3) | data formatting | bytes 2621440
  53.9 0.0 copy-done
  53.9 0.8 %copy.16 = bf16[128,2048]{1,0:T(8,128)(2,1)} copy(bf16[128,2048]{1,0:T(8,128)(2,1)S(1)} %copy-done) | data formatting | bytes 1048576
Async XLA Ops:
  51.4 2.5 %copy-start = (bf16[128,2048]{1,0:T(8,128)(2,1)S(1)}, bf16[128,2048]{1,0:T(8,128)(2,1)}, u32[]{:S(2)}) copy-start(bf16[128,2048]{1,0:T(8,128)(2,1)} %get-tuple-element.9) | copy-start | bytes 1572868

commit v3 on v2

--- a/solution.py
+++ b/solution.py
@@ -66,6 +66,10 @@
     part_sem,
     out_send,
     out_recv,
+    relay_buf,
+    slot_out,
+    slot_in,
+    relay_sem,
 ):
     section, seq, mp = lax.axis_index("section"), lax.axis_index("seq"), lax.axis_index("mp")
     owner_count = sections * seqs
@@ -253,47 +257,93 @@
 
     lax.fori_loop(second_hops, hops, relay, 0)
 
-    def out_copy(owner, g):
+    far_seq = lax.rem(seq + hops, seqs)
+    partner = section * seqs + far_seq
+    near_first = lax.div(seq, hops) * hops
+    slot_out[...] = jnp.zeros(slot_out.shape, jnp.int32)
+    slot_out[0:1, 0:tokens] = slot_row
+
+    def to_partner(source, target, at_sem):
         return pltpu.make_async_remote_copy(
-            src_ref=outgoing.at[g, owner],
-            dst_ref=delivered_hbm.at[me, :, pl.ds(g * width, width)],
-            send_sem=out_send.at[g, owner],
-            recv_sem=out_recv.at[g, me],
+            src_ref=source,
+            dst_ref=target,
+            send_sem=relay_sem.at[0, at_sem],
+            recv_sem=relay_sem.at[1, at_sem],
+            device_id=at(section, far_seq, mp),
+            device_id_type=MESH,
+        )
+
+    slot_copy = to_partner(slot_out, slot_in, 2)
+    slot_copy.start()
+
+    def landing(source, g):
+        return delivered_hbm.at[source, :, pl.ds(g * width, width)]
+
+    def out_copy(source, spot_at, owner, g):
+        return pltpu.make_async_remote_copy(
+            src_ref=outgoing.at[g, spot_at],
+            dst_ref=landing(source, g),
+            send_sem=out_send.at[g, spot_at],
+            recv_sem=out_recv.at[g, source],
             device_id=at(owner // seqs, lax.rem(owner, seqs), mp),
             device_id_type=MESH,
         )
 
-    def fill(owner, g):
-        spot = jnp.where(slot_at + owner * capacity == slot_row, 1.0, 0.0).astype(BF16)
-        outgoing[g, owner] = jnp.dot(
-            spot,
-            normed_buf[g * tokens : (g + 1) * tokens, :],
-            preferred_element_type=F32,
-        ).astype(BF16)
+    def fill(slots, block, owner, spot_at, g):
+        spot = jnp.where(slot_at + owner * capacity == slots, 1.0, 0.0).astype(BF16)
+        outgoing[g, spot_at] = jnp.dot(spot, block, preferred_element_type=F32).astype(BF16)
+
+    def near(k):
+        sec = lax.rem(section + k, sections)
+        ring = lax.rem(lax.rem(seq, hops) + lax.div(k, sections), hops)
+        owner = sec * seqs + near_first + ring
+        return owner, sec * seqs + lax.rem(near_first + ring + hops, seqs)
 
     keeps = []
+
+    def keep_own(source, spot_at, g):
+        keep = pltpu.make_async_copy(
+            outgoing.at[g, spot_at], landing(source, g), out_send.at[g, spot_at]
+        )
+        keep.start()
+        keeps.append(keep)
+
+    relay_copies = [slot_copy]
     for g in range(2):
         part_copies[g].wait_recv()
         residual = own_part[g * tokens : (g + 1) * tokens] + part_recv[g].astype(F32)
         normed_buf[g * tokens : (g + 1) * tokens, :] = rms_scale(
             residual, merge_ref[...].reshape(1, width)
         ).astype(BF16)
+        relay_copy = to_partner(
+            normed_buf.at[pl.ds(g * tokens, tokens)], relay_buf.at[g], g
+        )
+        relay_copy.start()
+        relay_copies.append(relay_copy)
 
         def send_out(k, carry):
-            owner = lax.rem(me + k, owner_count)
-            fill(owner, g)
-            out_copy(owner, g).start()
+            owner, _ = near(k)
+            fill(slot_row, normed_buf[g * tokens : (g + 1) * tokens, :], owner, owner, g)
+            out_copy(me, owner, owner, g).start()
             return carry
 
-        lax.fori_loop(1, owner_count, send_out, 0)
-        fill(me, g)
-        keep = pltpu.make_async_copy(
-            outgoing.at[g, me],
-            delivered_hbm.at[me, :, pl.ds(g * width, width)],
-            out_send.at[g, me],
-        )
-        keep.start()
-        keeps.append(keep)
+        lax.fori_loop(1, hops * sections, send_out, 0)
+        fill(slot_row, normed_buf[g * tokens : (g + 1) * tokens, :], me, me, g)
+        keep_own(me, me, g)
+
+    slot_copy.wait_recv()
+    for g in range(2):
+        relay_copies[1 + g].wait_recv()
+
+        def pass_on(k, carry):
+            owner, spot_at = near(k)
+            fill(slot_in[0:1, 0:tokens], relay_buf[g], owner, spot_at, g)
+            out_copy(partner, spot_at, owner, g).start()
+            return carry
+
+        lax.fori_loop(1, hops * sections, pass_on, 0)
+        fill(slot_in[0:1, 0:tokens], relay_buf[g], me, partner, g)
+        keep_own(partner, partner, g)
 
     def side_arrival(j, carry):
         block = side - 2 * j
@@ -367,18 +417,21 @@
     for keep in keeps:
         keep.wait()
 
+    for relay_copy in relay_copies:
+        relay_copy.wait_send()
+
     def finish_out(k, carry):
-        owner = lax.rem(me + k, owner_count)
+        owner, spot_at = near(k)
         for g in range(2):
-            out_copy(owner, g).wait_send()
-            pltpu.make_async_copy(
-                outgoing.at[g, owner],
-                delivered_hbm.at[owner, :, pl.ds(g * width, width)],
-                out_recv.at[g, owner],
-            ).wait()
-        return carry
-
-    lax.fori_loop(1, owner_count, finish_out, 0)
+            out_copy(me, owner, owner, g).wait_send()
+            out_copy(partner, spot_at, owner, g).wait_send()
+            for source in (owner, spot_at):
+                pltpu.make_async_copy(
+                    outgoing.at[g, source], landing(source, g), out_recv.at[g, source]
+                ).wait()
+        return carry
+
+    lax.fori_loop(1, hops * sections, finish_out, 0)
 
 
 def per_device(
@@ -443,6 +496,10 @@
             pltpu.SemaphoreType.DMA((2, 2)),
             pltpu.SemaphoreType.DMA((2, owner_count)),
             pltpu.SemaphoreType.DMA((2, owner_count)),
+            pltpu.VMEM((2, tokens, width), BF16),
+            pltpu.VMEM((8, 128), jnp.int32),
+            pltpu.VMEM((8, 128), jnp.int32),
+            pltpu.SemaphoreType.DMA((2, 3)),
         ],
         compiler_params=pltpu.CompilerParams(
             collective_id=0, has_side_effects=True, vmem_limit_bytes=56 * 1024 * 1024

time: 54.9 us -> 49.3 us (0.90)
  Pallas kernels: 50.8 us -> 45.2 us
    pallas_call x1, Pallas kernels: 50.8 us -> 45.2 us  [per_device(): pl.pallas_call(functools.partial(kernel, sections, seqs, capacity), out_s...]
where the time goes in v3:
time: 49.3 us; the launch traced here: 49.2 us
  Pallas kernels  45.2 us (92%)
  local copies, waits for them, and re-layouts  3.31 us (7%)
  between operations  0.65 us (1%)
    pallas_call x1, Pallas kernels, per_device(): pl.pallas_call(functools.partial(kernel, sections, seqs, capacity), out_s...  45.2 us
    unnamed x4, local copies, waits for them, and re-layouts  3.31 us

profile of v3, /device:TPU:0, one launch (start us, length us, event | category | flops | bytes accessed | tf_op | source)
XLA Modules:
  0.0 49.2 jit_solution(18287818832914649493)
XLA Ops:
  0.6 45.2 %shard_map.122 = (bf16[16,16,2560]{2,1,0:T(8,128)(2,1)}, bf16[128,2048]{1,0:T(8,128)(2,1)}) custom-call(bf16[256,1280]{1,0:T(8,128)(2,1)} %patches_ref.1, bf16[3,1280,640]{2,1,0:T(8,128)(2,1)} %inner_hbm.1, f32[1280]{0:T(1024)} %norm_ref.1, bf16[640,1280]{1,0:T(8,128)(2,1)} %outer_hbm.1, f32[1280]{0:T(1024)} %merge_ref.1, s32[1,256]{1,0:T(1,128)} %window_ref.1, ...), custom_call_target="tpu_custom_call" | custom-call | tf_op jit(solution)/shard_map/pallas_call | solution.py:461
  45.8 0.0 copy-start
  45.8 2.5 %copy.15 = bf16[256,2560]{1,0:T(8,128)(2,1)} copy(bf16[256,2560]{1,0:T(8,128)(2,1)} %bitcast.3) | data formatting | bytes 2621440
  48.4 0.0 copy-done
  48.4 0.8 %copy.16 = bf16[128,2048]{1,0:T(8,128)(2,1)} copy(bf16[128,2048]{1,0:T(8,128)(2,1)S(1)} %copy-done) | data formatting | bytes 1048576
Async XLA Ops:
  45.8 2.5 %copy-start = (bf16[128,2048]{1,0:T(8,128)(2,1)S(1)}, bf16[128,2048]{1,0:T(8,128)(2,1)}, u32[]{:S(2)}) copy-start(bf16[128,2048]{1,0:T(8,128)(2,1)} %get-tuple-element.9) | copy-start | bytes 1572868
